TPU v7x, 32 devices: a whole 2x2x4 slice. The times are simulated.
32 devices in a mesh: group: 2 (over y), phi: 4 (over z), row: 2 (over core), gz: 2 (over x).
Axes of the slice: x: 2, y: 2, z: 4, core: 2. Of those that a mesh axis runs over, the one named last changes fastest.
Arguments:
- source_field: float32 [3, 128, 32, 256], P(None, ('group', 'phi'), 'gz', 'row'), parts along dimension 1, may hold values from -6 to 6
- labels: int32 [128, 32, 256], P(('group', 'phi'), 'gz', 'row'), parts along dimension 0, may hold values from 0 to 2
Outputs:
- potential: float32 [128, 32, 256], P(('group', 'phi'), 'gz', 'row'), parts along dimension 0
There are 2 independent parts, one for each index of `group`. A program takes and returns all parts, laid end to end along the dimension named above; each array names one. Nothing has to cross between parts.
Inputs may be any that keep to these rules, and one draw needn't show every extreme that they name: `labels`: 0 is air, 1 iron, 2 coil pack.
All inputs are finite; a program needn't handle non-finite values.
Results may differ from a plain program's by a relative error of at most 0.0001.
Values sent between devices are 32-bit elements; how exact they have to be, the bound alone decides.
A program may use at most 64 MiB of HBM per device.

v0:
```python
import jax
import jax.numpy as jnp
from jax import lax
from jax.sharding import PartitionSpec as P

ITERS = 4


iron_perm = 40.0
iron_sat = 0.25
coil_perm = 4.0
coil_sat = 1.0
step_cap = 0.1
spectral = 0.9


def extended(cells, sides, width):
    for axis, dim in sides:
        count = lax.axis_size(axis)
        head = lax.slice_in_dim(cells, 0, width, axis=dim)
        tail = lax.slice_in_dim(cells, cells.shape[dim] - width, cells.shape[dim], axis=dim)
        cells = jnp.concatenate(
            [
                lax.ppermute(tail, axis, [(i, (i + 1) % count) for i in range(count)]),
                cells,
                lax.ppermute(head, axis, [((i + 1) % count, i) for i in range(count)]),
            ],
            axis=dim,
        )
    return cells


def chebyshev_weights(sweep_count):
    weights = [1.0]
    weights.append(1.0 / (1.0 - spectral * spectral / 2.0))
    while len(weights) < sweep_count:
        weights.append(1.0 / (1.0 - spectral * spectral * weights[-1] / 4.0))
    return weights


def neighbor(values, axis_dim, offset):
    leading = values.ndim - 3
    picks = [slice(None)] * leading
    for position in range(3):
        begin = 1 + (offset if position == axis_dim else 0)
        length = values.shape[leading + position] - 2
        picks.append(slice(begin, begin + length))
    return values[tuple(picks)]


def close_rims(values, axial_dim, radial_dim, depth):
    row_place = lax.axis_index("row")
    row_count = lax.axis_size("row")
    axial_place = lax.axis_index("gz")
    axial_count = lax.axis_size("gz")
    radial_iota = lax.broadcasted_iota(jnp.int32, values.shape, radial_dim)
    axial_iota = lax.broadcasted_iota(jnp.int32, values.shape, axial_dim)
    radial_last = values.shape[radial_dim] - 1
    axial_last = values.shape[axial_dim] - 1
    outside = (radial_iota < depth) & (row_place == 0) | (radial_iota > radial_last - depth) & (
        row_place == row_count - 1
    )
    outside = (
        outside
        | (axial_iota < depth) & (axial_place == 0)
        | (axial_iota > axial_last - depth) & (axial_place == axial_count - 1)
    )
    return jnp.where(outside, jnp.zeros_like(values), values)


def field_terms(padded, source_field, labels):
    field_sq = jnp.zeros(labels.shape, jnp.float32)
    for axis_dim in range(3):
        gradient = 0.5 * (neighbor(padded, axis_dim, 1) - neighbor(padded, axis_dim, -1))
        total_field = source_field[axis_dim] - gradient
        field_sq = field_sq + total_field * total_field
    iron_value = 1.0 + (iron_perm - 1.0) / (1.0 + field_sq / iron_sat)
    coil_value = 1.0 + (coil_perm - 1.0) / (1.0 + field_sq / coil_sat)
    perm = jnp.where(labels == 1, iron_value, jnp.where(labels == 2, coil_value, 1.0))
    return jnp.concatenate([(perm - 1.0)[None], perm[None] * source_field], axis=0)


def relax(padded, field_pad):
    perm_pad = 1.0 + field_pad[0]
    perm_here = neighbor(perm_pad, 0, 0)
    numerator = jnp.zeros(perm_here.shape, jnp.float32)
    denominator = jnp.zeros(perm_here.shape, jnp.float32)
    for axis_dim in range(3):
        flux_pad = field_pad[1 + axis_dim]
        flux_here = neighbor(flux_pad, axis_dim, 0)
        for offset in (1, -1):
            perm_there = neighbor(perm_pad, axis_dim, offset)
            conduct = 2.0 * perm_here * perm_there / (perm_here + perm_there)
            source_flux = offset * 0.5 * (flux_here + neighbor(flux_pad, axis_dim, offset))
            numerator = numerator + conduct * neighbor(padded, axis_dim, offset) - source_flux
            denominator = denominator + conduct
    return numerator / denominator


def on_device(source_field, labels):
    weights = chebyshev_weights(ITERS)
    shape_phi, shape_z, shape_r = labels.shape
    cell_count = (
        shape_phi
        * shape_z
        * shape_r
        * lax.axis_size("phi")
        * lax.axis_size("row")
        * lax.axis_size("gz")
    )
    depth = 1
    potential = jnp.zeros(labels.shape, jnp.float32)
    earlier = potential
    padded = jnp.zeros(
        (shape_phi + 2 * depth, shape_z + 2 * depth, shape_r + 2 * depth), jnp.float32
    )
    for sweep_index in range(ITERS):
        inner = padded
        stacked = field_terms(padded, source_field, labels)
        field_pad = extended(stacked, (("phi", 1), ("row", 3), ("gz", 2)), 1)
        field_pad = close_rims(field_pad, 2, 3, 1)
        relaxed = relax(inner, field_pad)
        update = earlier + weights[sweep_index] * (relaxed - earlier) - potential
        more_sweeps = sweep_index + 1 < ITERS
        sum_squares = lax.psum(jnp.sum(update * update), ("phi", "row", "gz"))
        factor = jnp.minimum(1.0, step_cap / jnp.sqrt(sum_squares / cell_count + 1e-06))
        earlier = potential
        potential = potential + factor * update
        if more_sweeps:
            padded = extended(potential, (("phi", 0), ("row", 2), ("gz", 1)), depth)
            padded = close_rims(padded, 1, 2, depth)
    return potential


def solution(mesh):
    placed = (P(None, ("group", "phi"), "gz", "row"), P(("group", "phi"), "gz", "row"))
    return jax.shard_map(
        on_device,
        mesh=mesh,
        in_specs=placed,
        out_specs=P(("group", "phi"), "gz", "row"),
        check_vma=False,
    )
```

profile of v0, /device:TPU:0, one launch (start us, length us, event | category | flops | bytes accessed | tf_op | source)
XLA Modules:
  0.0 253.3 jit_solution(10699831640470339875)
XLA Ops:
  2.3 3.1 %collective-permute-start = (f32[4,1,16,128]{3,2,1,0:T(8,128)S(1)}, f32[4,1,16,128]{3,2,1,0:T(8,128)S(1)}, u32[]{:S(2)}, u32[]{:S(2)}) collective-permute-start(f32[4,1,16,128]{3,2,1,0:T(8,128)S(1)} %get-tuple-element.61), channel_id=1, source_target_pairs={{0,4},{4,8},{8,12},{12,0},{1,5},{5,9},{9,13},{13,1},{2,6},{6,10},{... | collective-permute-start | bytes 98312 | tf_op jit(solution)/shard_map/ppermute | solution.py:24
  5.3 2.1 collective-permute-start.1
  7.4 1.9 collective-permute-done
  15.9 2.9 %collective-permute-done.4 = f32[4,18,1,130]{3,2,1,0:T(1,128)S(1)} collective-permute-done((f32[4,18,1,130]{3,2,1,0:T(1,128)S(1)}, f32[4,18,1,130]{3,2,1,0:T(1,128)S(1)}, u32[]{:S(2)}, u32[]{:S(2)}) %collective-permute-start.4) | collective-permute-done | bytes 37472 | tf_op jit(solution)/shard_map/ppermute | solution.py:24
  22.2 33.9 %psum.28 = f32[]{:T(128)} all-reduce(f32[]{:T(128)} %get-tuple-element.17), channel_id=1, replica_groups=mesh['group'=2,'phi'=4,'row'=2,'gz'=2] {'phi','row','gz'}, use_global_device_ids=true, to_apply=%region_1.2 | all-reduce | flops 1 | bytes 8 | tf_op jit(solution)/shard_map/psum | solution.py:125
  56.8 3.8 %collective-permute-start.7 = (f32[1,16,128]{2,1,0:T(8,128)S(1)}, f32[1,16,128]{2,1,0:T(8,128)S(1)}, u32[]{:S(2)}, u32[]{:S(2)}) collective-permute-start(f32[1,16,128]{2,1,0:T(8,128)S(1)} %get-tuple-element.80), channel_id=1, source_target_pairs={{4,0},{8,4},{12,8},{0,12},{5,1},{9,5},{13,9},{1,13},{6,2},{10,6},{... | collective-permute-start | bytes 24584 | tf_op jit(solution)/shard_map/ppermute | solution.py:26
  64.3 2.0 collective-permute-start.11
  68.9 3.9 %collective-permute-start.13 = (f32[4,1,16,128]{3,2,1,0:T(8,128)S(1)}, f32[4,1,16,128]{3,2,1,0:T(8,128)S(1)}, u32[]{:S(2)}, u32[]{:S(2)}) collective-permute-start(f32[4,1,16,128]{3,2,1,0:T(8,128)S(1)} %get-tuple-element.60), channel_id=1, source_target_pairs={{4,0},{8,4},{12,8},{0,12},{5,1},{9,5},{13,9},{1,13},{6,2},{10,6},{... | collective-permute-start | bytes 98312 | tf_op jit(solution)/shard_map/ppermute | solution.py:26
  72.8 2.1 collective-permute-done.12
  80.7 2.8 %collective-permute-done.16 = f32[4,18,1,130]{3,2,1,0:T(1,128)S(1)} collective-permute-done((f32[4,18,1,130]{3,2,1,0:T(1,128)S(1)}, f32[4,18,1,130]{3,2,1,0:T(1,128)S(1)}, u32[]{:S(2)}, u32[]{:S(2)}) %collective-permute-start.16) | collective-permute-done | bytes 37472 | tf_op jit(solution)/shard_map/ppermute | solution.py:24
  87.1 34.1 %psum.29 = f32[]{:T(128)} all-reduce(f32[]{:T(128)} %get-tuple-element.13), channel_id=1, replica_groups=mesh['group'=2,'phi'=4,'row'=2,'gz'=2] {'phi','row','gz'}, use_global_device_ids=true, to_apply=%region_3.4 | all-reduce | flops 1 | bytes 8 | tf_op jit(solution)/shard_map/psum | solution.py:125
  122.1 3.8 %collective-permute-start.19 = (f32[1,16,128]{2,1,0:T(8,128)S(1)}, f32[1,16,128]{2,1,0:T(8,128)S(1)}, u32[]{:S(2)}, u32[]{:S(2)}) collective-permute-start(f32[1,16,128]{2,1,0:T(8,128)S(1)} %get-tuple-element.78), channel_id=1, source_target_pairs={{4,0},{8,4},{12,8},{0,12},{5,1},{9,5},{13,9},{1,13},{6,2},{10,6},{... | collective-permute-start | bytes 24584 | tf_op jit(solution)/shard_map/ppermute | solution.py:26
  129.5 2.0 collective-permute-start.23
  131.6 1.7 collective-permute-done.22
  134.2 4.1 %collective-permute-start.25 = (f32[4,1,16,128]{3,2,1,0:T(8,128)S(1)}, f32[4,1,16,128]{3,2,1,0:T(8,128)S(1)}, u32[]{:S(2)}, u32[]{:S(2)}) collective-permute-start(f32[4,1,16,128]{3,2,1,0:T(8,128)S(1)} %get-tuple-element.58), channel_id=1, source_target_pairs={{4,0},{8,4},{12,8},{0,12},{5,1},{9,5},{13,9},{1,13},{6,2},{10,6},{... | collective-permute-start | bytes 98312 | tf_op jit(solution)/shard_map/ppermute | solution.py:26
  138.2 1.9 collective-permute-done.24
  145.9 2.8 %collective-permute-done.28 = f32[4,18,1,130]{3,2,1,0:T(1,128)S(1)} collective-permute-done((f32[4,18,1,130]{3,2,1,0:T(1,128)S(1)}, f32[4,18,1,130]{3,2,1,0:T(1,128)S(1)}, u32[]{:S(2)}, u32[]{:S(2)}) %collective-permute-start.28) | collective-permute-done | bytes 37472 | tf_op jit(solution)/shard_map/ppermute | solution.py:24
  152.4 34.3 %psum.30 = f32[]{:T(128)} all-reduce(f32[]{:T(128)} %get-tuple-element.9), channel_id=1, replica_groups=mesh['group'=2,'phi'=4,'row'=2,'gz'=2] {'phi','row','gz'}, use_global_device_ids=true, to_apply=%region_5.6 | all-reduce | flops 1 | bytes 8 | tf_op jit(solution)/shard_map/psum | solution.py:125
  187.5 3.8 %collective-permute-start.31 = (f32[1,16,128]{2,1,0:T(8,128)S(1)}, f32[1,16,128]{2,1,0:T(8,128)S(1)}, u32[]{:S(2)}, u32[]{:S(2)}) collective-permute-start(f32[1,16,128]{2,1,0:T(8,128)S(1)} %get-tuple-element.76), channel_id=1, source_target_pairs={{4,0},{8,4},{12,8},{0,12},{5,1},{9,5},{13,9},{1,13},{6,2},{10,6},{... | collective-permute-start | bytes 24584 | tf_op jit(solution)/shard_map/ppermute | solution.py:26
  194.9 2.0 collective-permute-start.35
  199.6 3.9 %collective-permute-start.37 = (f32[4,1,16,128]{3,2,1,0:T(8,128)S(1)}, f32[4,1,16,128]{3,2,1,0:T(8,128)S(1)}, u32[]{:S(2)}, u32[]{:S(2)}) collective-permute-start(f32[4,1,16,128]{3,2,1,0:T(8,128)S(1)} %get-tuple-element.56), channel_id=1, source_target_pairs={{4,0},{8,4},{12,8},{0,12},{5,1},{9,5},{13,9},{1,13},{6,2},{10,6},{... | collective-permute-start | bytes 98312 | tf_op jit(solution)/shard_map/ppermute | solution.py:26
  203.4 2.1 collective-permute-done.36
  211.3 2.8 %collective-permute-done.40 = f32[4,18,1,130]{3,2,1,0:T(1,128)S(1)} collective-permute-done((f32[4,18,1,130]{3,2,1,0:T(1,128)S(1)}, f32[4,18,1,130]{3,2,1,0:T(1,128)S(1)}, u32[]{:S(2)}, u32[]{:S(2)}) %collective-permute-start.40) | collective-permute-done | bytes 37472 | tf_op jit(solution)/shard_map/ppermute | solution.py:24
  217.8 34.1 %psum.31 = f32[]{:T(128)} all-reduce(f32[]{:T(128)} %get-tuple-element.5), channel_id=1, replica_groups=mesh['group'=2,'phi'=4,'row'=2,'gz'=2] {'phi','row','gz'}, use_global_device_ids=true, to_apply=%region_7.8 | all-reduce | flops 1 | bytes 8 | tf_op jit(solution)/shard_map/psum | solution.py:125
  (139 shorter events, 58.0 us)
Async XLA Ops:
  2.3 7.1 %collective-permute-start = (f32[4,1,16,128]{3,2,1,0:T(8,128)S(1)}, f32[4,1,16,128]{3,2,1,0:T(8,128)S(1)}, u32[]{:S(2)}, u32[]{:S(2)}) collective-permute-start(f32[4,1,16,128]{3,2,1,0:T(8,128)S(1)} %get-tuple-element.61), channel_id=1, source_target_pairs={{0,4},{4,8},{8,12},{12,0},{1,5},{5,9},{9,13},{13,1},{2,6},{6,10},{... | collective-permute-start | bytes 98312 | tf_op jit(solution)/shard_map/ppermute | solution.py:24
  5.3 4.3 %collective-permute-start.1 = (f32[4,1,16,128]{3,2,1,0:T(8,128)S(1)}, f32[4,1,16,128]{3,2,1,0:T(8,128)S(1)}, u32[]{:S(2)}, u32[]{:S(2)}) collective-permute-start(f32[4,1,16,128]{3,2,1,0:T(8,128)S(1)} %get-tuple-element.62), channel_id=1, source_target_pairs={{4,0},{8,4},{12,8},{0,12},{5,1},{9,5},{13,9},{1,13},{6,2},{10,6},{... | collective-permute-start | bytes 98312 | tf_op jit(solution)/shard_map/ppermute | solution.py:26
  13.8 5.0 %collective-permute-start.4 = (f32[4,18,1,130]{3,2,1,0:T(1,128)S(1)}, f32[4,18,1,130]{3,2,1,0:T(1,128)S(1)}, u32[]{:S(2)}, u32[]{:S(2)}) collective-permute-start(f32[4,18,1,130]{3,2,1,0:T(1,128)S(1)} %get-tuple-element.45), channel_id=1, source_target_pairs={{0,1},{1,0},{2,3},{3,2},{4,5},{5,4},{6,7},{7,6},{8,9},{9,8},{10,11... | collective-permute-start | bytes 112328 | tf_op jit(solution)/shard_map/ppermute | solution.py:24
  15.4 4.6 %collective-permute-start.5 = (f32[4,18,1,130]{3,2,1,0:T(1,128)S(1)}, f32[4,18,1,130]{3,2,1,0:T(1,128)S(1)}, u32[]{:S(2)}, u32[]{:S(2)}) collective-permute-start(f32[4,18,1,130]{3,2,1,0:T(1,128)S(1)} %get-tuple-element.46), channel_id=1, source_target_pairs={{1,0},{0,1},{3,2},{2,3},{5,4},{4,5},{7,6},{6,7},{9,8},{8,9},{11,10... | collective-permute-start | bytes 112328 | tf_op jit(solution)/shard_map/ppermute | solution.py:26
  56.8 5.5 %collective-permute-start.6 = (f32[1,16,128]{2,1,0:T(8,128)S(1)}, f32[1,16,128]{2,1,0:T(8,128)S(1)}, u32[]{:S(2)}, u32[]{:S(2)}) collective-permute-start(f32[1,16,128]{2,1,0:T(8,128)S(1)} %get-tuple-element.79), channel_id=1, source_target_pairs={{0,4},{4,8},{8,12},{12,0},{1,5},{5,9},{9,13},{13,1},{2,6},{6,10},{... | collective-permute-start | bytes 24584 | tf_op jit(solution)/shard_map/ppermute | solution.py:24
  56.8 5.4 %collective-permute-start.7 = (f32[1,16,128]{2,1,0:T(8,128)S(1)}, f32[1,16,128]{2,1,0:T(8,128)S(1)}, u32[]{:S(2)}, u32[]{:S(2)}) collective-permute-start(f32[1,16,128]{2,1,0:T(8,128)S(1)} %get-tuple-element.80), channel_id=1, source_target_pairs={{4,0},{8,4},{12,8},{0,12},{5,1},{9,5},{13,9},{1,13},{6,2},{10,6},{... | collective-permute-start | bytes 24584 | tf_op jit(solution)/shard_map/ppermute | solution.py:26
  64.3 4.0 %collective-permute-start.11 = (f32[18,1,130]{2,1,0:T(1,128)S(1)}, f32[18,1,130]{2,1,0:T(1,128)S(1)}, u32[]{:S(2)}, u32[]{:S(2)}) collective-permute-start(f32[18,1,130]{2,1,0:T(1,128)S(1)} %get-tuple-element.68), channel_id=1, source_target_pairs={{1,0},{0,1},{3,2},{2,3},{5,4},{4,5},{7,6},{6,7},{9,8},{8,9},{11,10... | collective-permute-start | bytes 28088 | tf_op jit(solution)/shard_map/ppermute | solution.py:26
  68.8 6.0 %collective-permute-start.12 = (f32[4,1,16,128]{3,2,1,0:T(8,128)S(1)}, f32[4,1,16,128]{3,2,1,0:T(8,128)S(1)}, u32[]{:S(2)}, u32[]{:S(2)}) collective-permute-start(f32[4,1,16,128]{3,2,1,0:T(8,128)S(1)} %get-tuple-element.59), channel_id=1, source_target_pairs={{0,4},{4,8},{8,12},{12,0},{1,5},{5,9},{9,13},{13,1},{2,6},{6,10},{... | collective-permute-start | bytes 98312 | tf_op jit(solution)/shard_map/ppermute | solution.py:24
  68.9 6.0 %collective-permute-start.13 = (f32[4,1,16,128]{3,2,1,0:T(8,128)S(1)}, f32[4,1,16,128]{3,2,1,0:T(8,128)S(1)}, u32[]{:S(2)}, u32[]{:S(2)}) collective-permute-start(f32[4,1,16,128]{3,2,1,0:T(8,128)S(1)} %get-tuple-element.60), channel_id=1, source_target_pairs={{4,0},{8,4},{12,8},{0,12},{5,1},{9,5},{13,9},{1,13},{6,2},{10,6},{... | collective-permute-start | bytes 98312 | tf_op jit(solution)/shard_map/ppermute | solution.py:26
  78.6 4.9 %collective-permute-start.16 = (f32[4,18,1,130]{3,2,1,0:T(1,128)S(1)}, f32[4,18,1,130]{3,2,1,0:T(1,128)S(1)}, u32[]{:S(2)}, u32[]{:S(2)}) collective-permute-start(f32[4,18,1,130]{3,2,1,0:T(1,128)S(1)} %get-tuple-element.39), channel_id=1, source_target_pairs={{0,1},{1,0},{2,3},{3,2},{4,5},{5,4},{6,7},{7,6},{8,9},{9,8},{10,11... | collective-permute-start | bytes 112328 | tf_op jit(solution)/shard_map/ppermute | solution.py:24
  80.2 4.5 %collective-permute-start.17 = (f32[4,18,1,130]{3,2,1,0:T(1,128)S(1)}, f32[4,18,1,130]{3,2,1,0:T(1,128)S(1)}, u32[]{:S(2)}, u32[]{:S(2)}) collective-permute-start(f32[4,18,1,130]{3,2,1,0:T(1,128)S(1)} %get-tuple-element.40), channel_id=1, source_target_pairs={{1,0},{0,1},{3,2},{2,3},{5,4},{4,5},{7,6},{6,7},{9,8},{8,9},{11,10... | collective-permute-start | bytes 112328 | tf_op jit(solution)/shard_map/ppermute | solution.py:26
  122.0 5.5 %collective-permute-start.18 = (f32[1,16,128]{2,1,0:T(8,128)S(1)}, f32[1,16,128]{2,1,0:T(8,128)S(1)}, u32[]{:S(2)}, u32[]{:S(2)}) collective-permute-start(f32[1,16,128]{2,1,0:T(8,128)S(1)} %get-tuple-element.77), channel_id=1, source_target_pairs={{0,4},{4,8},{8,12},{12,0},{1,5},{5,9},{9,13},{13,1},{2,6},{6,10},{... | collective-permute-start | bytes 24584 | tf_op jit(solution)/shard_map/ppermute | solution.py:24
  122.1 5.4 %collective-permute-start.19 = (f32[1,16,128]{2,1,0:T(8,128)S(1)}, f32[1,16,128]{2,1,0:T(8,128)S(1)}, u32[]{:S(2)}, u32[]{:S(2)}) collective-permute-start(f32[1,16,128]{2,1,0:T(8,128)S(1)} %get-tuple-element.78), channel_id=1, source_target_pairs={{4,0},{8,4},{12,8},{0,12},{5,1},{9,5},{13,9},{1,13},{6,2},{10,6},{... | collective-permute-start | bytes 24584 | tf_op jit(solution)/shard_map/ppermute | solution.py:26
  129.5 4.0 %collective-permute-start.23 = (f32[18,1,130]{2,1,0:T(1,128)S(1)}, f32[18,1,130]{2,1,0:T(1,128)S(1)}, u32[]{:S(2)}, u32[]{:S(2)}) collective-permute-start(f32[18,1,130]{2,1,0:T(1,128)S(1)} %get-tuple-element.66), channel_id=1, source_target_pairs={{1,0},{0,1},{3,2},{2,3},{5,4},{4,5},{7,6},{6,7},{9,8},{8,9},{11,10... | collective-permute-start | bytes 28088 | tf_op jit(solution)/shard_map/ppermute | solution.py:26
  134.1 6.0 %collective-permute-start.24 = (f32[4,1,16,128]{3,2,1,0:T(8,128)S(1)}, f32[4,1,16,128]{3,2,1,0:T(8,128)S(1)}, u32[]{:S(2)}, u32[]{:S(2)}) collective-permute-start(f32[4,1,16,128]{3,2,1,0:T(8,128)S(1)} %get-tuple-element.57), channel_id=1, source_target_pairs={{0,4},{4,8},{8,12},{12,0},{1,5},{5,9},{9,13},{13,1},{2,6},{6,10},{... | collective-permute-start | bytes 98312 | tf_op jit(solution)/shard_map/ppermute | solution.py:24
  134.2 6.0 %collective-permute-start.25 = (f32[4,1,16,128]{3,2,1,0:T(8,128)S(1)}, f32[4,1,16,128]{3,2,1,0:T(8,128)S(1)}, u32[]{:S(2)}, u32[]{:S(2)}) collective-permute-start(f32[4,1,16,128]{3,2,1,0:T(8,128)S(1)} %get-tuple-element.58), channel_id=1, source_target_pairs={{4,0},{8,4},{12,8},{0,12},{5,1},{9,5},{13,9},{1,13},{6,2},{10,6},{... | collective-permute-start | bytes 98312 | tf_op jit(solution)/shard_map/ppermute | solution.py:26
  143.8 4.9 %collective-permute-start.28 = (f32[4,18,1,130]{3,2,1,0:T(1,128)S(1)}, f32[4,18,1,130]{3,2,1,0:T(1,128)S(1)}, u32[]{:S(2)}, u32[]{:S(2)}) collective-permute-start(f32[4,18,1,130]{3,2,1,0:T(1,128)S(1)} %get-tuple-element.33), channel_id=1, source_target_pairs={{0,1},{1,0},{2,3},{3,2},{4,5},{5,4},{6,7},{7,6},{8,9},{9,8},{10,11... | collective-permute-start | bytes 112328 | tf_op jit(solution)/shard_map/ppermute | solution.py:24
  145.5 4.5 %collective-permute-start.29 = (f32[4,18,1,130]{3,2,1,0:T(1,128)S(1)}, f32[4,18,1,130]{3,2,1,0:T(1,128)S(1)}, u32[]{:S(2)}, u32[]{:S(2)}) collective-permute-start(f32[4,18,1,130]{3,2,1,0:T(1,128)S(1)} %get-tuple-element.34), channel_id=1, source_target_pairs={{1,0},{0,1},{3,2},{2,3},{5,4},{4,5},{7,6},{6,7},{9,8},{8,9},{11,10... | collective-permute-start | bytes 112328 | tf_op jit(solution)/shard_map/ppermute | solution.py:26
  187.4 5.5 %collective-permute-start.30 = (f32[1,16,128]{2,1,0:T(8,128)S(1)}, f32[1,16,128]{2,1,0:T(8,128)S(1)}, u32[]{:S(2)}, u32[]{:S(2)}) collective-permute-start(f32[1,16,128]{2,1,0:T(8,128)S(1)} %get-tuple-element.75), channel_id=1, source_target_pairs={{0,4},{4,8},{8,12},{12,0},{1,5},{5,9},{9,13},{13,1},{2,6},{6,10},{... | collective-permute-start | bytes 24584 | tf_op jit(solution)/shard_map/ppermute | solution.py:24
  187.5 5.4 %collective-permute-start.31 = (f32[1,16,128]{2,1,0:T(8,128)S(1)}, f32[1,16,128]{2,1,0:T(8,128)S(1)}, u32[]{:S(2)}, u32[]{:S(2)}) collective-permute-start(f32[1,16,128]{2,1,0:T(8,128)S(1)} %get-tuple-element.76), channel_id=1, source_target_pairs={{4,0},{8,4},{12,8},{0,12},{5,1},{9,5},{13,9},{1,13},{6,2},{10,6},{... | collective-permute-start | bytes 24584 | tf_op jit(solution)/shard_map/ppermute | solution.py:26
  199.5 6.0 %collective-permute-start.36 = (f32[4,1,16,128]{3,2,1,0:T(8,128)S(1)}, f32[4,1,16,128]{3,2,1,0:T(8,128)S(1)}, u32[]{:S(2)}, u32[]{:S(2)}) collective-permute-start(f32[4,1,16,128]{3,2,1,0:T(8,128)S(1)} %get-tuple-element.55), channel_id=1, source_target_pairs={{0,4},{4,8},{8,12},{12,0},{1,5},{5,9},{9,13},{13,1},{2,6},{6,10},{... | collective-permute-start | bytes 98312 | tf_op jit(solution)/shard_map/ppermute | solution.py:24
  199.6 6.0 %collective-permute-start.37 = (f32[4,1,16,128]{3,2,1,0:T(8,128)S(1)}, f32[4,1,16,128]{3,2,1,0:T(8,128)S(1)}, u32[]{:S(2)}, u32[]{:S(2)}) collective-permute-start(f32[4,1,16,128]{3,2,1,0:T(8,128)S(1)} %get-tuple-element.56), channel_id=1, source_target_pairs={{4,0},{8,4},{12,8},{0,12},{5,1},{9,5},{13,9},{1,13},{6,2},{10,6},{... | collective-permute-start | bytes 98312 | tf_op jit(solution)/shard_map/ppermute | solution.py:26
  209.2 4.9 %collective-permute-start.40 = (f32[4,18,1,130]{3,2,1,0:T(1,128)S(1)}, f32[4,18,1,130]{3,2,1,0:T(1,128)S(1)}, u32[]{:S(2)}, u32[]{:S(2)}) collective-permute-start(f32[4,18,1,130]{3,2,1,0:T(1,128)S(1)} %get-tuple-element.27), channel_id=1, source_target_pairs={{0,1},{1,0},{2,3},{3,2},{4,5},{5,4},{6,7},{7,6},{8,9},{9,8},{10,11... | collective-permute-start | bytes 112328 | tf_op jit(solution)/shard_map/ppermute | solution.py:24
  210.9 4.5 %collective-permute-start.41 = (f32[4,18,1,130]{3,2,1,0:T(1,128)S(1)}, f32[4,18,1,130]{3,2,1,0:T(1,128)S(1)}, u32[]{:S(2)}, u32[]{:S(2)}) collective-permute-start(f32[4,18,1,130]{3,2,1,0:T(1,128)S(1)} %get-tuple-element.28), channel_id=1, source_target_pairs={{1,0},{0,1},{3,2},{2,3},{5,4},{4,5},{7,6},{6,7},{9,8},{8,9},{11,10... | collective-permute-start | bytes 112328 | tf_op jit(solution)/shard_map/ppermute | solution.py:26
  (19 other events, 82.0 us)
where the time goes:
time: 254 us; the launch traced here: 253 us
  blocking collectives  136 us (54%)
  starting transfers between devices  47.4 us (19%)
  waiting for transfers between devices  40.4 us (16%)
  other arithmetic  16.8 us (7%)
  local copies, waits for them, and re-layouts  9.06 us (4%)
  between operations  3.26 us (1%)
    psum x4, blocking collectives, on_device(): sum_squares = lax.psum(jnp.sum(update * update), ('phi', 'row', 'gz'))  136 us
    ppermute x21, starting transfers between devices, extended(): lax.ppermute(head, axis, [((i + 1) % count, i) for i in range(count)])  36.4 us
    ppermute x21, waiting for transfers between devices, extended(): lax.ppermute(tail, axis, [(i, (i + 1) % count) for i in range(count)])  33.4 us
    ppermute x21, starting transfers between devices, extended(): lax.ppermute(tail, axis, [(i, (i + 1) % count) for i in range(count)])  10.9 us
    ppermute x21, waiting for transfers between devices, extended(): lax.ppermute(head, axis, [((i + 1) % count, i) for i in range(count)])  6.93 us
    reduce_sum x4, other arithmetic, on_device(): sum_squares = lax.psum(jnp.sum(update * update), ('phi', 'row', 'gz'))  5.15 us
  transfers between devices with their start and end apart: 42, of which 35 were waited for; matrix products, arithmetic and copies ran while one was open for 1% of the time, Pallas kernels for 0%

commit v1 on v0

v1 whole, which is shorter than its diff:
```python
import jax
import jax.numpy as jnp
from jax import lax
from jax.experimental import pallas as pl
from jax.experimental.pallas import tpu as pltpu
from jax.sharding import PartitionSpec as P

ITERS = 4
iron_perm = 40.0
iron_sat = 0.25
coil_perm = 4.0
coil_sat = 1.0
step_cap = 0.1
spectral = 0.9
MESH = pl.DeviceIdType.MESH


def chebyshev_weights(sweep_count):
    weights = [1.0]
    weights.append(1.0 / (1.0 - spectral * spectral / 2.0))
    while len(weights) < sweep_count:
        weights.append(1.0 / (1.0 - spectral * spectral * weights[-1] / 4.0))
    return weights


def make_kernel(n_phi, n_row, n_gz, shape):
    s_phi, s_z, s_r = shape
    peers = n_phi * n_row * n_gz
    half = s_phi // 2
    wide = 2 * s_r
    tall = s_z + 8
    cell_count = s_phi * s_z * s_r * peers
    weights = chebyshev_weights(ITERS)
    first, last = 2, half + 1

    def kernel(src, lab, out, S, L, A, B, Pot, M, U, G, FP, FU, sum_sem, halo_send, halo_recv, in_send, in_recv, loc_sem):
        p = lax.axis_index("phi")
        c = lax.axis_index("row")
        g = lax.axis_index("gz")
        me = (p * n_row + c) * n_gz + g
        lanes = pl.ds(pl.multiple_of(c * s_r, s_r), s_r)
        sib = 1 - c

        def own_part(core):
            return pl.ds((half - 1) * core, half + 1), pl.ds(2 - core, half + 1)

        def cut(ref, rows, z):
            return ref.at[:, rows, z, :] if ref is src else ref.at[rows, z, :]

        def land(ref, rows, z):
            return ref.at[:, rows, z, lanes] if ref is S else ref.at[rows, z, lanes]

        whole_z = pl.ds(0, s_z)
        local = []
        for n, (a, b) in enumerate(((src, S), (lab, L))):
            frm, to = own_part(c)
            copy = pltpu.make_async_copy(cut(a, frm, whole_z), land(b, to, whole_z), loc_sem.at[n])
            copy.start()
            local.append(copy)

        def peer(j):
            t = lax.rem(me + j, peers)
            return {"phi": t // (n_row * n_gz), "row": lax.rem(t // n_gz, n_row), "gz": lax.rem(t, n_gz)}

        rim = pl.ds(s_z, 8)
        S[:, :, rim, :] = jnp.zeros((3, half + 4, 8, wide), jnp.float32)
        L[:, rim, :] = jnp.zeros((half + 4, 8, wide), jnp.int32)
        for k in range(ITERS - 1):
            U[k, :, rim, :] = jnp.zeros((half + 4, 8, wide), jnp.float32)

        barrier = pltpu.get_barrier_semaphore()

        def greet(j, carry):
            pl.semaphore_signal(barrier, inc=1, device_id=peer(j), device_id_type=MESH)
            return carry

        lax.fori_loop(1, peers, greet, 0)
        pl.semaphore_wait(barrier, peers - 1)

        up_p, down_p = lax.rem(p + 1, n_phi), lax.rem(p + n_phi - 1, n_phi)
        has_up, has_down = g < n_gz - 1, g > 0
        up_g, down_g = jnp.minimum(g + 1, n_gz - 1), jnp.maximum(g - 1, 0)

        always, when_up, when_down = [], [], []
        for n, (a, b) in enumerate(((src, S), (lab, L))):
            def remote(frm, to, send, recv, where, n=n):
                return pltpu.make_async_remote_copy(
                    src_ref=frm, dst_ref=to, send_sem=in_send.at[n, send], recv_sem=in_recv.at[n, recv],
                    device_id=where, device_id_type=MESH)

            frm, to = own_part(sib)
            always.append(remote(cut(a, pl.ds(s_phi - 1, 1), whole_z), land(b, pl.ds(1, 1), whole_z), 1, 1 + c,
                                 {"phi": up_p, "row": 0}))
            always.append(remote(cut(a, pl.ds(0, 1), whole_z), land(b, pl.ds(last + 1, 1), whole_z), 2, 1 + c,
                                 {"phi": down_p, "row": 1}))
            always.append(remote(cut(a, frm, whole_z), land(b, to, whole_z), 0, 0, {"row": sib}))
            for t in range(2):
                rows = pl.ds(half * t, half)
                when_up.append(remote(cut(a, rows, pl.ds(s_z - 1, 1)), land(b, pl.ds(first, half), pl.ds(tall - 1, 1)),
                                      3 + t, 3 + c, {"gz": up_g, "row": t}))
                when_down.append(remote(cut(a, rows, pl.ds(0, 1)), land(b, pl.ds(first, half), pl.ds(s_z, 1)),
                                        5 + t, 5 + c, {"gz": down_g, "row": t}))

        def start_all(copies):
            for copy in copies:
                copy.start()

        def send_wait_all(copies):
            for copy in copies:
                copy.wait_send()

        @pl.when(has_up)
        def _():
            start_all(when_up)

        @pl.when(has_down)
        def _():
            start_all(when_down)

        start_all(always)

        def arrived(b, n, slot, rows, z, ln):
            ref = b.at[:, rows, z, ln] if b is S else b.at[rows, z, ln]
            pltpu.make_async_remote_copy(
                src_ref=ref, dst_ref=ref, send_sem=in_send.at[n, 0], recv_sem=in_recv.at[n, slot],
                device_id={"row": sib}, device_id_type=MESH).wait_recv()

        for copy in local:
            copy.wait()
        for n, b in enumerate((S, L)):
            frm, to = own_part(c)
            arrived(b, n, 0, to, whole_z, pl.ds(pl.multiple_of(sib * s_r, s_r), s_r))
            for core in range(2):
                arrived(b, n, 1 + core, pl.ds(jnp.where(c == 0, 1, last + 1), 1), whole_z, pl.ds(core * s_r, s_r))

        @pl.when(has_down)
        def _():
            for n, b in enumerate((S, L)):
                for core in range(2):
                    arrived(b, n, 3 + core, pl.ds(first, half), pl.ds(tall - 1, 1), pl.ds(core * s_r, s_r))

        @pl.when(has_up)
        def _():
            for n, b in enumerate((S, L)):
                for core in range(2):
                    arrived(b, n, 5 + core, pl.ds(first, half), pl.ds(s_z, 1), pl.ds(core * s_r, s_r))

        lane = lax.broadcasted_iota(jnp.int32, (tall, wide), 1)
        at_end, at_start = lane == wide - 1, lane == 0

        def z_up(x):
            return pltpu.roll(x, tall - 1, 0)

        def z_down(x):
            return pltpu.roll(x, 1, 0)

        def r_up(x, edge):
            return jnp.where(at_end[: x.shape[0]], edge, pltpu.roll(x, wide - 1, 1))

        def r_down(x, edge):
            return jnp.where(at_start[: x.shape[0]], edge, pltpu.roll(x, 1, 1))

        def conduct(a, b):
            return 2.0 * a * b / (a + b)

        q_up = {"phi": jnp.where(c == 1, up_p, p), "row": sib}
        q_down = {"phi": jnp.where(c == 0, down_p, p), "row": sib}
        z_top, z_low = pl.ds(s_z - 2, 2), pl.ds(0, 2)
        at_low, at_top = pl.ds(tall - 2, 2), pl.ds(s_z, 2)

        def halo(k, slot):
            def ref(rows, z):
                return U.at[k, rows, z, :]

            own = pl.ds(first, half)
            frm, to, where = (
                (ref(pl.ds(last - 1, 2), whole_z), ref(pl.ds(0, 2), whole_z), q_up),
                (ref(pl.ds(first, 2), whole_z), ref(pl.ds(last + 1, 2), whole_z), q_down),
                (ref(own, z_top), ref(own, at_low), {"gz": up_g}),
                (ref(own, z_low), ref(own, at_top), {"gz": down_g}),
                (ref(pl.ds(last, 1), z_top), ref(pl.ds(1, 1), at_low), dict(q_up, gz=up_g)),
                (ref(pl.ds(first, 1), z_top), ref(pl.ds(last + 1, 1), at_low), dict(q_down, gz=up_g)),
                (ref(pl.ds(last, 1), z_low), ref(pl.ds(1, 1), at_top), dict(q_up, gz=down_g)),
                (ref(pl.ds(first, 1), z_low), ref(pl.ds(last + 1, 1), at_top), dict(q_down, gz=down_g)),
            )[slot]
            return pltpu.make_async_remote_copy(
                src_ref=frm, dst_ref=to, send_sem=halo_send.at[k, slot], recv_sem=halo_recv.at[k, slot],
                device_id=where, device_id_type=MESH)

        UP, DOWN, BOTH = (2, 4, 5), (3, 6, 7), (0, 1)

        def halo_start(k):
            @pl.when(has_up)
            def _():
                start_all([halo(k, s) for s in UP])

            @pl.when(has_down)
            def _():
                start_all([halo(k, s) for s in DOWN])

            start_all([halo(k, s) for s in BOTH])

        def halo_arrive(k):
            for s in BOTH:
                halo(k, s).wait_recv()

            @pl.when(has_down)
            def _():
                for s in UP:
                    halo(k, s).wait_recv()

            @pl.when(has_up)
            def _():
                for s in DOWN:
                    halo(k, s).wait_recv()

        def halo_sent(k):
            send_wait_all([halo(k, s) for s in BOTH])

            @pl.when(has_up)
            def _():
                send_wait_all([halo(k, s) for s in UP])

            @pl.when(has_down)
            def _():
                send_wait_all([halo(k, s) for s in DOWN])

        def swap(frm, to, slot):
            return pltpu.make_async_remote_copy(
                src_ref=frm, dst_ref=to, send_sem=halo_send.at[ITERS - 1, slot], recv_sem=halo_recv.at[ITERS - 1, slot],
                device_id={"row": sib}, device_id_type=MESH)

        other_lanes = pl.ds(pl.multiple_of(sib * s_r, s_r), s_r)
        own_rows = pl.ds(first, half)

        def total_wait(k):
            return pltpu.make_async_remote_copy(
                src_ref=G.at[k, pl.ds(1, peers - 1)], dst_ref=G.at[k, pl.ds(1, peers - 1)],
                send_sem=sum_sem.at[0, k], recv_sem=sum_sem.at[1, k], device_id={"row": sib}, device_id_type=MESH)

        for k in range(ITERS):
            cur = k % 2

            def perm_row(i, carry, k=k, cur=cur):
                if k == 0:
                    label = L[i]
                    a = jnp.where(label == 1, iron_perm - 1.0, jnp.where(label == 2, coil_perm - 1.0, 0.0))
                    b = jnp.where(label == 1, 1.0 / iron_sat, jnp.where(label == 2, 1.0 / coil_sat, 0.0))
                    A[i] = a
                    B[i] = b
                    s0, s1, s2 = S[0, i], S[1, i], S[2, i]
                else:
                    a, b = A[i], B[i]
                    here = Pot[cur, i]
                    s0 = S[0, i] - 0.5 * (Pot[cur, i + 1] - Pot[cur, i - 1])
                    s1 = S[1, i] - 0.5 * (z_up(here) - z_down(here))
                    s2 = S[2, i] - 0.5 * (r_up(here, 0.0) - r_down(here, 0.0))
                field_sq = s0 * s0 + s1 * s1 + s2 * s2
                M[i] = 1.0 + a / (1.0 + field_sq * b)
                return carry

            lax.fori_loop(1, half + 3, perm_row, 0)

            def relax_row(i, carry, k=k, cur=cur):
                below, acc = carry
                m = M[i]
                mi = m[:s_z]
                above = conduct(mi, M[i + 1, :s_z])
                cz = conduct(m, z_up(m))
                cz_low = z_down(cz)[:s_z]
                cz = cz[:s_z]
                cr = conduct(mi, r_up(mi, 1.0))
                cr_low = conduct(mi, r_down(mi, 1.0))
                fz = m * S[1, i]
                fr = mi * S[2, i, :s_z]
                flux = M[i + 1, :s_z] * S[0, i + 1, :s_z] - M[i - 1, :s_z] * S[0, i - 1, :s_z]
                flux = flux + (z_up(fz) - z_down(fz))[:s_z] + (r_up(fr, 0.0) - r_down(fr, 0.0))
                numerator = -0.5 * flux
                if k > 0:
                    here = Pot[cur, i]
                    hi = here[:s_z]
                    numerator = (numerator + above * Pot[cur, i + 1, :s_z] + below * Pot[cur, i - 1, :s_z]
                                 + cz * z_up(here)[:s_z] + cz_low * z_down(here)[:s_z]
                                 + cr * r_up(hi, 0.0) + cr_low * r_down(hi, 0.0))
                relaxed = numerator / (above + below + cz + cz_low + cr + cr_low)
                if k == 0:
                    update = weights[0] * relaxed
                elif k == 1:
                    update = weights[1] * relaxed - hi
                else:
                    earlier = Pot[1 - cur, i, :s_z]
                    update = earlier + weights[k] * (relaxed - earlier) - hi
                U[k, i, :s_z] = update
                return above, acc + update * update

            start = conduct(M[1, :s_z], M[2, :s_z])
            _, acc = lax.fori_loop(first, last + 1, relax_row, (start, jnp.zeros((s_z, wide), jnp.float32)))

            if k < ITERS - 1:
                halo_start(k)
            else:
                give_update = swap(U.at[k, own_rows, whole_z, other_lanes], FU, 1)
                give_update.start()
            acc = acc[:, :s_r] + acc[:, s_r:]
            part = acc[:8]
            for z in range(8, s_z, 8):
                part = part + acc[z : z + 8]
            G[k, 0] = part

            def share(j, carry, k=k):
                pltpu.make_async_remote_copy(
                    src_ref=G.at[k, 0], dst_ref=G.at[k, peers - j], send_sem=sum_sem.at[0, k],
                    recv_sem=sum_sem.at[1, k], device_id=peer(j), device_id_type=MESH).start()
                return carry

            lax.fori_loop(1, peers, share, 0)
            total_wait(k).wait_recv()
            sum_squares = jnp.sum(jnp.sum(G[k], axis=0), keepdims=True)
            factor = jnp.minimum(1.0, step_cap / jnp.sqrt(sum_squares / cell_count + 1e-06))

            if k < ITERS - 1:
                halo_arrive(k)
                wide_factor = jnp.broadcast_to(factor, (tall, wide))

                def step(i, carry, k=k, cur=cur):
                    new = wide_factor * U[k, i]
                    if k > 0:
                        new = new + Pot[cur, i]
                    Pot[1 - cur, i] = new
                    return carry

                lax.fori_loop(0, half + 4, step, 0)
                if k == ITERS - 2:
                    give_potential = swap(Pot.at[1 - cur, own_rows, whole_z, other_lanes], FP, 0)
                    give_potential.start()
            else:
                wide_factor = jnp.broadcast_to(factor, (half, s_z, s_r))
                out[pl.ds(half * c, half)] = (
                    Pot[cur, first : last + 1, :s_z, lanes] + wide_factor * U[k, first : last + 1, :s_z, lanes])
                give_potential.wait_recv()
                give_update.wait_recv()
                out[pl.ds(half * sib, half)] = FP[...] + wide_factor * FU[...]

        send_wait_all(always)

        @pl.when(has_up)
        def _():
            send_wait_all(when_up)

        @pl.when(has_down)
        def _():
            send_wait_all(when_down)

        for k in range(ITERS):
            total_wait(k).wait_send()
            if k < ITERS - 1:
                halo_sent(k)
        give_potential.wait_send()
        give_update.wait_send()

    rows = half + 4
    scratch = [
        pltpu.VMEM((3, rows, tall, wide), jnp.float32),
        pltpu.VMEM((rows, tall, wide), jnp.int32),
        pltpu.VMEM((rows, tall, wide), jnp.float32),
        pltpu.VMEM((rows, tall, wide), jnp.float32),
        pltpu.VMEM((2, rows, tall, wide), jnp.float32),
        pltpu.VMEM((rows, tall, wide), jnp.float32),
        pltpu.VMEM((ITERS, rows, tall, wide), jnp.float32),
        pltpu.VMEM((ITERS, peers, 8, s_r), jnp.float32),
        pltpu.VMEM((half, s_z, s_r), jnp.float32),
        pltpu.VMEM((half, s_z, s_r), jnp.float32),
        pltpu.SemaphoreType.DMA((2, ITERS)),
        pltpu.SemaphoreType.DMA((ITERS, 8)),
        pltpu.SemaphoreType.DMA((ITERS, 8)),
        pltpu.SemaphoreType.DMA((2, 7)),
        pltpu.SemaphoreType.DMA((2, 7)),
        pltpu.SemaphoreType.DMA((2,)),
    ]
    return pl.pallas_call(
        kernel,
        out_shape=jax.ShapeDtypeStruct(shape, jnp.float32),
        in_specs=[pl.BlockSpec(memory_space=pl.ANY)] * 2,
        out_specs=pl.BlockSpec(memory_space=pltpu.VMEM),
        scratch_shapes=scratch,
        compiler_params=pltpu.CompilerParams(
            collective_id=0, has_side_effects=True, vmem_limit_bytes=24 * 1024 * 1024),
        name="sweeps",
    )


def solution(mesh):
    sizes = mesh.shape

    def on_device(source_field, labels):
        return make_kernel(sizes["phi"], sizes["row"], sizes["gz"], labels.shape)(source_field, labels)

    placed = (P(None, ("group", "phi"), "gz", "row"), P(("group", "phi"), "gz", "row"))
    return jax.shard_map(
        on_device,
        mesh=mesh,
        in_specs=placed,
        out_specs=P(("group", "phi"), "gz", "row"),
        check_vma=False,
    )
```

time: 254 us -> 39 us (0.15)
  blocking collectives: 136 us -> 0 us
  starting transfers between devices: 47.4 us -> 0 us
  waiting for transfers between devices: 40.4 us -> 0 us
  Pallas kernels: 0 us -> 36.3 us
  other arithmetic: 16.8 us -> 0 us
  local copies, waits for them, and re-layouts: 9.06 us -> 2.56 us
  between operations: 3.26 us -> 0.01 us
    psum x4 -> x0, blocking collectives: 136 us -> none  [on_device(): sum_squares = lax.psum(jnp.sum(update * update), ('phi', 'row', 'gz'))]
    ppermute x42 -> x0, starting transfers between devices: 47.4 us -> none  [the longest x21 36.4 us: extended(): lax.ppermute(head, axis, [((i + 1) % count, i) for i in range(count)])]
    ppermute x42 -> x0, waiting for transfers between devices: 40.4 us -> none  [the longest x21 33.4 us: extended(): lax.ppermute(tail, axis, [(i, (i + 1) % count) for i in range(count)])]
    pallas_call x0 -> x1, Pallas kernels: none -> 36.3 us  [on_device(): make_kernel(sizes['phi'], sizes['row'], sizes['gz'], labels.shape)]
    reduce_sum x4 -> x0, other arithmetic: 5.15 us -> none  [on_device(): sum_squares = lax.psum(jnp.sum(update * update), ('phi', 'row', 'gz'))]
    select_n x7 -> x0, other arithmetic: 4.23 us -> none  [close_rims(): return jnp.where(outside, jnp.zeros_like(values), values)]
    ppermute x8 -> x0, local copies, waits for them, and re-layouts: 3.97 us -> none  [the longest x4 1.99 us: extended(): lax.ppermute(head, axis, [((i + 1) % count, i) for i in range(count)])]
    slice x11 -> x0, other arithmetic: 2.68 us -> none  [extended(): lax.slice_in_dim(cells, cells.shape[dim] - width, cells.shape[dim], axis=...]
  transfers between devices with their start and end apart: 42 -> 0, of which waited for: 35 -> 0; matrix products, arithmetic and copies ran while one was open for 1% -> 0% of each run, Pallas kernels for 0% -> 0%
where the time goes in v1:
time: 39 us; the launch traced here: 38.9 us
  Pallas kernels  36.3 us (93%)
  local copies, waits for them, and re-layouts  2.56 us (7%)
    pallas_call x1, Pallas kernels, on_device(): make_kernel(sizes['phi'], sizes['row'], sizes['gz'], labels.shape)  36.3 us
    unnamed x5, local copies, waits for them, and re-layouts  2.56 us

profile of v1, /device:TPU:0, one launch (start us, length us, event | category | flops | bytes accessed | tf_op | source)
XLA Modules:
  0.0 38.9 jit_solution(6777300407186327359)
XLA Ops:
  0.0 0.0 copy-start
  0.0 1.0 %copy-done = f32[3,16,16,128]{3,2,1,0:T(8,128)S(1)} copy-done((f32[3,16,16,128]{3,2,1,0:T(8,128)S(1)}, f32[3,16,16,128]{3,2,1,0:T(8,128)}, u32[]{:S(2)}) %copy-start) | copy-done | bytes 393240
  1.0 0.0 copy-start.1
  1.0 0.9 %copy-done.1 = s32[16,16,128]{2,1,0:T(8,128)S(1)} copy-done((s32[16,16,128]{2,1,0:T(8,128)S(1)}, s32[16,16,128]{2,1,0:T(8,128)}, u32[]{:S(2)}) %copy-start.1) | copy-done | bytes 131096
  1.9 36.3 %sweeps.1 = f32[16,16,128]{2,1,0:T(8,128)S(1)} custom-call(f32[3,16,16,128]{3,2,1,0:T(8,128)S(1)} %copy-done, s32[16,16,128]{2,1,0:T(8,128)S(1)} %copy-done.1), custom_call_target="tpu_custom_call" | custom-call | tf_op jit(solution)/shard_map/sweeps/pallas_call | solution.py:396
  38.2 0.7 %copy.4 = f32[16,16,128]{2,1,0:T(8,128)} copy(f32[16,16,128]{2,1,0:T(8,128)S(1)} %sweeps.1) | data formatting | bytes 262144
Async XLA Ops:
  0.0 1.0 %copy-start = (f32[3,16,16,128]{3,2,1,0:T(8,128)S(1)}, f32[3,16,16,128]{3,2,1,0:T(8,128)}, u32[]{:S(2)}) copy-start(f32[3,16,16,128]{3,2,1,0:T(8,128)} %src.1) | copy-start | bytes 1179652
  1.0 0.9 %copy-start.1 = (s32[16,16,128]{2,1,0:T(8,128)S(1)}, s32[16,16,128]{2,1,0:T(8,128)}, u32[]{:S(2)}) copy-start(s32[16,16,128]{2,1,0:T(8,128)} %lab.1) | copy-start | bytes 393220

commit v2 on v1

--- a/solution.py
+++ b/solution.py
@@ -33,11 +33,10 @@
     weights = chebyshev_weights(ITERS)
     first, last = 2, half + 1
 
-    def kernel(src, lab, out, S, L, A, B, Pot, M, U, G, FP, FU, sum_sem, halo_send, halo_recv, in_send, in_recv, loc_sem):
+    def kernel(src, lab, out, S, L, A, B, Pot, M, U, G, FP, FU, X, XL, sum_sem, halo_send, halo_recv, in_send, in_recv, loc_sem):
         p = lax.axis_index("phi")
         c = lax.axis_index("row")
         g = lax.axis_index("gz")
-        me = (p * n_row + c) * n_gz + g
         lanes = pl.ds(pl.multiple_of(c * s_r, s_r), s_r)
         sib = 1 - c
 
@@ -45,22 +44,40 @@
             return pl.ds((half - 1) * core, half + 1), pl.ds(2 - core, half + 1)
 
         def cut(ref, rows, z):
-            return ref.at[:, rows, z, :] if ref is src else ref.at[rows, z, :]
+            return ref.at[:, rows, z, :] if ref is src or ref is X else ref.at[rows, z, :]
 
         def land(ref, rows, z):
             return ref.at[:, rows, z, lanes] if ref is S else ref.at[rows, z, lanes]
 
         whole_z = pl.ds(0, s_z)
-        local = []
-        for n, (a, b) in enumerate(((src, S), (lab, L))):
+        local, stages = [], []
+        for n, (a, b, staged) in enumerate(((src, S, X), (lab, L, XL))):
+            stage = pltpu.make_async_copy(a, staged, loc_sem.at[2 + n])
+            stage.start()
+            stages.append(stage)
             frm, to = own_part(c)
             copy = pltpu.make_async_copy(cut(a, frm, whole_z), land(b, to, whole_z), loc_sem.at[n])
             copy.start()
             local.append(copy)
 
         def peer(j):
-            t = lax.rem(me + j, peers)
-            return {"phi": t // (n_row * n_gz), "row": lax.rem(t // n_gz, n_row), "gz": lax.rem(t, n_gz)}
+            return {
+                "phi": lax.rem(p + j // (n_row * n_gz), n_phi),
+                "row": lax.rem(c + (j // n_gz) % n_row, n_row),
+                "gz": lax.rem(g + j % n_gz, n_gz),
+            }
+
+        def each_peer(body):
+            if peers > 32:
+                lax.fori_loop(1, peers, lambda j, carry: (body(j, peer(j)), carry)[1], 0)
+            else:
+                for j, where in peer_list:
+                    body(j, where)
+
+        if peers <= 32:
+            per_chip = n_row * n_gz
+            order = sorted(range(1, peers), key=lambda j: -min(j // per_chip, n_phi - j // per_chip))
+            peer_list = [(j, peer(j)) for j in order]
 
         rim = pl.ds(s_z, 8)
         S[:, :, rim, :] = jnp.zeros((3, half + 4, 8, wide), jnp.float32)
@@ -70,19 +87,20 @@
 
         barrier = pltpu.get_barrier_semaphore()
 
-        def greet(j, carry):
-            pl.semaphore_signal(barrier, inc=1, device_id=peer(j), device_id_type=MESH)
-            return carry
-
-        lax.fori_loop(1, peers, greet, 0)
+        def greet(j, where):
+            pl.semaphore_signal(barrier, inc=1, device_id=where, device_id_type=MESH)
+
+        each_peer(greet)
         pl.semaphore_wait(barrier, peers - 1)
 
+        for stage in stages:
+            stage.wait()
         up_p, down_p = lax.rem(p + 1, n_phi), lax.rem(p + n_phi - 1, n_phi)
         has_up, has_down = g < n_gz - 1, g > 0
         up_g, down_g = jnp.minimum(g + 1, n_gz - 1), jnp.maximum(g - 1, 0)
 
         always, when_up, when_down = [], [], []
-        for n, (a, b) in enumerate(((src, S), (lab, L))):
+        for n, (a, b) in enumerate(((X, S), (XL, L))):
             def remote(frm, to, send, recv, where, n=n):
                 return pltpu.make_async_remote_copy(
                     src_ref=frm, dst_ref=to, send_sem=in_send.at[n, send], recv_sem=in_recv.at[n, recv],
@@ -259,7 +277,7 @@
                 M[i] = 1.0 + a / (1.0 + field_sq * b)
                 return carry
 
-            lax.fori_loop(1, half + 3, perm_row, 0)
+            lax.fori_loop(1, half + 3, perm_row, 0, unroll=True)
 
             def relax_row(i, carry, k=k, cur=cur):
                 below, acc = carry
@@ -294,7 +312,7 @@
                 return above, acc + update * update
 
             start = conduct(M[1, :s_z], M[2, :s_z])
-            _, acc = lax.fori_loop(first, last + 1, relax_row, (start, jnp.zeros((s_z, wide), jnp.float32)))
+            _, acc = lax.fori_loop(first, last + 1, relax_row, (start, jnp.zeros((s_z, wide), jnp.float32)), unroll=True)
 
             if k < ITERS - 1:
                 halo_start(k)
@@ -305,18 +323,17 @@
             part = acc[:8]
             for z in range(8, s_z, 8):
                 part = part + acc[z : z + 8]
-            G[k, 0] = part
-
-            def share(j, carry, k=k):
+            G[k, 0:1] = jnp.sum(part, axis=0, keepdims=True)
+
+            def share(j, where, k=k):
                 pltpu.make_async_remote_copy(
-                    src_ref=G.at[k, 0], dst_ref=G.at[k, peers - j], send_sem=sum_sem.at[0, k],
-                    recv_sem=sum_sem.at[1, k], device_id=peer(j), device_id_type=MESH).start()
-                return carry
-
-            lax.fori_loop(1, peers, share, 0)
+                    src_ref=G.at[k, pl.ds(0, 1)], dst_ref=G.at[k, pl.ds(j, 1)], send_sem=sum_sem.at[0, k],
+                    recv_sem=sum_sem.at[1, k], device_id=where, device_id_type=MESH).start()
+
+            each_peer(share)
             total_wait(k).wait_recv()
-            sum_squares = jnp.sum(jnp.sum(G[k], axis=0), keepdims=True)
-            factor = jnp.minimum(1.0, step_cap / jnp.sqrt(sum_squares / cell_count + 1e-06))
+            sum_squares = jnp.sum(jnp.sum(G[k], axis=0, keepdims=True), axis=1, keepdims=True)
+            factor = jnp.minimum(1.0, step_cap * lax.rsqrt(sum_squares * (1.0 / cell_count) + 1e-06))
 
             if k < ITERS - 1:
                 halo_arrive(k)
@@ -329,7 +346,7 @@
                     Pot[1 - cur, i] = new
                     return carry
 
-                lax.fori_loop(0, half + 4, step, 0)
+                lax.fori_loop(0, half + 4, step, 0, unroll=True)
                 if k == ITERS - 2:
                     give_potential = swap(Pot.at[1 - cur, own_rows, whole_z, other_lanes], FP, 0)
                     give_potential.start()
@@ -367,20 +384,22 @@
         pltpu.VMEM((2, rows, tall, wide), jnp.float32),
         pltpu.VMEM((rows, tall, wide), jnp.float32),
         pltpu.VMEM((ITERS, rows, tall, wide), jnp.float32),
-        pltpu.VMEM((ITERS, peers, 8, s_r), jnp.float32),
+        pltpu.VMEM((ITERS, peers, s_r), jnp.float32),
         pltpu.VMEM((half, s_z, s_r), jnp.float32),
         pltpu.VMEM((half, s_z, s_r), jnp.float32),
+        pltpu.VMEM((3,) + tuple(shape), jnp.float32),
+        pltpu.VMEM(tuple(shape), jnp.int32),
         pltpu.SemaphoreType.DMA((2, ITERS)),
         pltpu.SemaphoreType.DMA((ITERS, 8)),
         pltpu.SemaphoreType.DMA((ITERS, 8)),
         pltpu.SemaphoreType.DMA((2, 7)),
         pltpu.SemaphoreType.DMA((2, 7)),
-        pltpu.SemaphoreType.DMA((2,)),
+        pltpu.SemaphoreType.DMA((4,)),
     ]
     return pl.pallas_call(
         kernel,
         out_shape=jax.ShapeDtypeStruct(shape, jnp.float32),
-        in_specs=[pl.BlockSpec(memory_space=pl.ANY)] * 2,
+        in_specs=[pl.BlockSpec(memory_space=pltpu.HBM)] * 2,
         out_specs=pl.BlockSpec(memory_space=pltpu.VMEM),
         scratch_shapes=scratch,
         compiler_params=pltpu.CompilerParams(

time: 39 us -> 32.5 us (0.83)
  Pallas kernels: 36.3 us -> 29.8 us
    pallas_call x1, Pallas kernels: 36.3 us -> 29.8 us  [on_device(): make_kernel(sizes['phi'], sizes['row'], sizes['gz'], labels.shape)]
where the time goes in v2:
time: 32.5 us; the launch traced here: 32.4 us
  Pallas kernels  29.8 us (92%)
  local copies, waits for them, and re-layouts  2.56 us (8%)
    pallas_call x1, Pallas kernels, on_device(): make_kernel(sizes['phi'], sizes['row'], sizes['gz'], labels.shape)  29.8 us
    unnamed x5, local copies, waits for them, and re-layouts  2.56 us

profile of v2, /device:TPU:0, one launch (start us, length us, event | category | flops | bytes accessed | tf_op | source)
XLA Modules:
  0.0 32.4 jit_solution(15782230963045967062)
XLA Ops:
  0.0 0.0 copy-start
  0.0 1.0 %copy-done = f32[3,16,16,128]{3,2,1,0:T(8,128)S(1)} copy-done((f32[3,16,16,128]{3,2,1,0:T(8,128)S(1)}, f32[3,16,16,128]{3,2,1,0:T(8,128)}, u32[]{:S(2)}) %copy-start) | copy-done | bytes 393240
  1.0 0.0 copy-start.1
  1.0 0.9 %copy-done.1 = s32[16,16,128]{2,1,0:T(8,128)S(1)} copy-done((s32[16,16,128]{2,1,0:T(8,128)S(1)}, s32[16,16,128]{2,1,0:T(8,128)}, u32[]{:S(2)}) %copy-start.1) | copy-done | bytes 131096
  1.9 29.8 %sweeps.1 = f32[16,16,128]{2,1,0:T(8,128)S(1)} custom-call(f32[3,16,16,128]{3,2,1,0:T(8,128)S(1)} %copy-done, s32[16,16,128]{2,1,0:T(8,128)S(1)} %copy-done.1), custom_call_target="tpu_custom_call" | custom-call | tf_op jit(solution)/shard_map/sweeps/pallas_call | solution.py:415
  31.7 0.7 %copy.4 = f32[16,16,128]{2,1,0:T(8,128)} copy(f32[16,16,128]{2,1,0:T(8,128)S(1)} %sweeps.1) | data formatting | bytes 262144
Async XLA Ops:
  0.0 1.0 %copy-start = (f32[3,16,16,128]{3,2,1,0:T(8,128)S(1)}, f32[3,16,16,128]{3,2,1,0:T(8,128)}, u32[]{:S(2)}) copy-start(f32[3,16,16,128]{3,2,1,0:T(8,128)} %src.1) | copy-start | bytes 1179652
  1.0 0.9 %copy-start.1 = (s32[16,16,128]{2,1,0:T(8,128)S(1)}, s32[16,16,128]{2,1,0:T(8,128)}, u32[]{:S(2)}) copy-start(s32[16,16,128]{2,1,0:T(8,128)} %lab.1) | copy-start | bytes 393220

commit v3 on v2

--- a/solution.py
+++ b/solution.py
@@ -127,6 +127,8 @@
             for copy in copies:
                 copy.wait_send()
 
+        start_all(always)
+
         @pl.when(has_up)
         def _():
             start_all(when_up)
@@ -134,8 +136,6 @@
         @pl.when(has_down)
         def _():
             start_all(when_down)
-
-        start_all(always)
 
         def arrived(b, n, slot, rows, z, ln):
             ref = b.at[:, rows, z, ln] if b is S else b.at[rows, z, ln]
@@ -143,13 +143,27 @@
                 src_ref=ref, dst_ref=ref, send_sem=in_send.at[n, 0], recv_sem=in_recv.at[n, slot],
                 device_id={"row": sib}, device_id_type=MESH).wait_recv()
 
+        def first_perm(i, z):
+            label = L[i, z]
+            a = jnp.where(label == 1, iron_perm - 1.0, jnp.where(label == 2, coil_perm - 1.0, 0.0))
+            b = jnp.where(label == 1, 1.0 / iron_sat, jnp.where(label == 2, 1.0 / coil_sat, 0.0))
+            A[i, z] = a
+            B[i, z] = b
+            s0, s1, s2 = S[0, i, z], S[1, i, z], S[2, i, z]
+            M[i, z] = 1.0 + a / (1.0 + (s0 * s0 + s1 * s1 + s2 * s2) * b)
+
         for copy in local:
             copy.wait()
         for n, b in enumerate((S, L)):
-            frm, to = own_part(c)
-            arrived(b, n, 0, to, whole_z, pl.ds(pl.multiple_of(sib * s_r, s_r), s_r))
+            arrived(b, n, 0, own_part(c)[1], whole_z, pl.ds(pl.multiple_of(sib * s_r, s_r), s_r))
+        for i in range(first, last + 1):
+            first_perm(i, whole_z)
+        near = jnp.where(c == 0, last + 1, 1)
+        first_perm(near, whole_z)
+        for n, b in enumerate((S, L)):
             for core in range(2):
                 arrived(b, n, 1 + core, pl.ds(jnp.where(c == 0, 1, last + 1), 1), whole_z, pl.ds(core * s_r, s_r))
+        first_perm(last + 2 - near, whole_z)
 
         @pl.when(has_down)
         def _():
@@ -162,6 +176,9 @@
             for n, b in enumerate((S, L)):
                 for core in range(2):
                     arrived(b, n, 5 + core, pl.ds(first, half), pl.ds(s_z, 1), pl.ds(core * s_r, s_r))
+
+        for i in range(1, last + 2):
+            first_perm(i, rim)
 
         lane = lax.broadcasted_iota(jnp.int32, (tall, wide), 1)
         at_end, at_start = lane == wide - 1, lane == 0
@@ -260,24 +277,17 @@
             cur = k % 2
 
             def perm_row(i, carry, k=k, cur=cur):
-                if k == 0:
-                    label = L[i]
-                    a = jnp.where(label == 1, iron_perm - 1.0, jnp.where(label == 2, coil_perm - 1.0, 0.0))
-                    b = jnp.where(label == 1, 1.0 / iron_sat, jnp.where(label == 2, 1.0 / coil_sat, 0.0))
-                    A[i] = a
-                    B[i] = b
-                    s0, s1, s2 = S[0, i], S[1, i], S[2, i]
-                else:
-                    a, b = A[i], B[i]
-                    here = Pot[cur, i]
-                    s0 = S[0, i] - 0.5 * (Pot[cur, i + 1] - Pot[cur, i - 1])
-                    s1 = S[1, i] - 0.5 * (z_up(here) - z_down(here))
-                    s2 = S[2, i] - 0.5 * (r_up(here, 0.0) - r_down(here, 0.0))
+                a, b = A[i], B[i]
+                here = Pot[cur, i]
+                s0 = S[0, i] - 0.5 * (Pot[cur, i + 1] - Pot[cur, i - 1])
+                s1 = S[1, i] - 0.5 * (z_up(here) - z_down(here))
+                s2 = S[2, i] - 0.5 * (r_up(here, 0.0) - r_down(here, 0.0))
                 field_sq = s0 * s0 + s1 * s1 + s2 * s2
                 M[i] = 1.0 + a / (1.0 + field_sq * b)
                 return carry
 
-            lax.fori_loop(1, half + 3, perm_row, 0, unroll=True)
+            if k > 0:
+                lax.fori_loop(1, half + 3, perm_row, 0, unroll=True)
 
             def relax_row(i, carry, k=k, cur=cur):
                 below, acc = carry
@@ -314,23 +324,23 @@
             start = conduct(M[1, :s_z], M[2, :s_z])
             _, acc = lax.fori_loop(first, last + 1, relax_row, (start, jnp.zeros((s_z, wide), jnp.float32)), unroll=True)
 
+            acc = acc[:, :s_r] + acc[:, s_r:]
+            part = acc[:8]
+            for z in range(8, s_z, 8):
+                part = part + acc[z : z + 8]
+            G[k, 0:1] = jnp.sum(part, axis=0, keepdims=True)
+
+            def share(j, where, k=k):
+                pltpu.make_async_remote_copy(
+                    src_ref=G.at[k, pl.ds(0, 1)], dst_ref=G.at[k, pl.ds(j, 1)], send_sem=sum_sem.at[0, k],
+                    recv_sem=sum_sem.at[1, k], device_id=where, device_id_type=MESH).start()
+
+            each_peer(share)
             if k < ITERS - 1:
                 halo_start(k)
             else:
                 give_update = swap(U.at[k, own_rows, whole_z, other_lanes], FU, 1)
                 give_update.start()
-            acc = acc[:, :s_r] + acc[:, s_r:]
-            part = acc[:8]
-            for z in range(8, s_z, 8):
-                part = part + acc[z : z + 8]
-            G[k, 0:1] = jnp.sum(part, axis=0, keepdims=True)
-
-            def share(j, where, k=k):
-                pltpu.make_async_remote_copy(
-                    src_ref=G.at[k, pl.ds(0, 1)], dst_ref=G.at[k, pl.ds(j, 1)], send_sem=sum_sem.at[0, k],
-                    recv_sem=sum_sem.at[1, k], device_id=where, device_id_type=MESH).start()
-
-            each_peer(share)
             total_wait(k).wait_recv()
             sum_squares = jnp.sum(jnp.sum(G[k], axis=0, keepdims=True), axis=1, keepdims=True)
             factor = jnp.minimum(1.0, step_cap * lax.rsqrt(sum_squares * (1.0 / cell_count) + 1e-06))

time: 32.5 us -> 31.3 us (0.963)
  Pallas kernels: 29.8 us -> 28.6 us
    pallas_call x1, Pallas kernels: 29.8 us -> 28.6 us  [on_device(): make_kernel(sizes['phi'], sizes['row'], sizes['gz'], labels.shape)]
where the time goes in v3:
time: 31.3 us; the launch traced here: 31.1 us
  Pallas kernels  28.6 us (91%)
  local copies, waits for them, and re-layouts  2.56 us (8%)
    pallas_call x1, Pallas kernels, on_device(): make_kernel(sizes['phi'], sizes['row'], sizes['gz'], labels.shape)  28.6 us
    unnamed x5, local copies, waits for them, and re-layouts  2.56 us

profile of v3, /device:TPU:0, one launch (start us, length us, event | category | flops | bytes accessed | tf_op | source)
XLA Modules:
  0.0 31.1 jit_solution(10586966182457029458)
XLA Ops:
  0.0 0.0 copy-start
  0.0 1.0 %copy-done = f32[3,16,16,128]{3,2,1,0:T(8,128)S(1)} copy-done((f32[3,16,16,128]{3,2,1,0:T(8,128)S(1)}, f32[3,16,16,128]{3,2,1,0:T(8,128)}, u32[]{:S(2)}) %copy-start) | copy-done | bytes 393240
  1.0 0.0 copy-start.1
  1.0 0.9 %copy-done.1 = s32[16,16,128]{2,1,0:T(8,128)S(1)} copy-done((s32[16,16,128]{2,1,0:T(8,128)S(1)}, s32[16,16,128]{2,1,0:T(8,128)}, u32[]{:S(2)}) %copy-start.1) | copy-done | bytes 131096
  1.9 28.6 %sweeps.1 = f32[16,16,128]{2,1,0:T(8,128)S(1)} custom-call(f32[3,16,16,128]{3,2,1,0:T(8,128)S(1)} %copy-done, s32[16,16,128]{2,1,0:T(8,128)S(1)} %copy-done.1), custom_call_target="tpu_custom_call" | custom-call | tf_op jit(solution)/shard_map/sweeps/pallas_call | solution.py:425
  30.5 0.7 %copy.4 = f32[16,16,128]{2,1,0:T(8,128)} copy(f32[16,16,128]{2,1,0:T(8,128)S(1)} %sweeps.1) | data formatting | bytes 262144
Async XLA Ops:
  0.0 1.0 %copy-start = (f32[3,16,16,128]{3,2,1,0:T(8,128)S(1)}, f32[3,16,16,128]{3,2,1,0:T(8,128)}, u32[]{:S(2)}) copy-start(f32[3,16,16,128]{3,2,1,0:T(8,128)} %src.1) | copy-start | bytes 1179652
  1.0 0.9 %copy-start.1 = (s32[16,16,128]{2,1,0:T(8,128)S(1)}, s32[16,16,128]{2,1,0:T(8,128)}, u32[]{:S(2)}) copy-start(s32[16,16,128]{2,1,0:T(8,128)} %lab.1) | copy-start | bytes 393220

commit v4 on v3

--- a/solution.py
+++ b/solution.py
@@ -60,9 +60,14 @@
             copy.start()
             local.append(copy)
 
+        def along_phi(d):
+            if n_phi == 4 and peers <= 32:
+                return (p, p + 1 - 2 * lax.rem(p, 2), lax.rem(p + 2, 4), 3 - p)[d]
+            return lax.rem(p + d, n_phi)
+
         def peer(j):
             return {
-                "phi": lax.rem(p + j // (n_row * n_gz), n_phi),
+                "phi": along_phi(j // (n_row * n_gz)),
                 "row": lax.rem(c + (j // n_gz) % n_row, n_row),
                 "gz": lax.rem(g + j % n_gz, n_gz),
             }
@@ -76,7 +81,7 @@
 
         if peers <= 32:
             per_chip = n_row * n_gz
-            order = sorted(range(1, peers), key=lambda j: -min(j // per_chip, n_phi - j // per_chip))
+            order = sorted(range(1, peers), key=lambda j: (-(j // per_chip), -(j % n_gz)))
             peer_list = [(j, peer(j)) for j in order]
 
         rim = pl.ds(s_z, 8)

time: 31.3 us -> 31.1 us (level)
  no operation moved by 1% of the time
where the time goes in v4:
time: 31.1 us; the launch traced here: 31 us
  Pallas kernels  28.4 us (91%)
  local copies, waits for them, and re-layouts  2.56 us (8%)
    pallas_call x1, Pallas kernels, on_device(): make_kernel(sizes['phi'], sizes['row'], sizes['gz'], labels.shape)  28.4 us
    unnamed x5, local copies, waits for them, and re-layouts  2.56 us

profile of v4, /device:TPU:0, one launch (start us, length us, event | category | flops | bytes accessed | tf_op | source)
XLA Modules:
  0.0 31.0 jit_solution(12075146039926367686)
XLA Ops:
  0.0 0.0 copy-start
  0.0 1.0 %copy-done = f32[3,16,16,128]{3,2,1,0:T(8,128)S(1)} copy-done((f32[3,16,16,128]{3,2,1,0:T(8,128)S(1)}, f32[3,16,16,128]{3,2,1,0:T(8,128)}, u32[]{:S(2)}) %copy-start) | copy-done | bytes 393240
  1.0 0.0 copy-start.1
  1.0 0.9 %copy-done.1 = s32[16,16,128]{2,1,0:T(8,128)S(1)} copy-done((s32[16,16,128]{2,1,0:T(8,128)S(1)}, s32[16,16,128]{2,1,0:T(8,128)}, u32[]{:S(2)}) %copy-start.1) | copy-done | bytes 131096
  1.9 28.4 %sweeps.1 = f32[16,16,128]{2,1,0:T(8,128)S(1)} custom-call(f32[3,16,16,128]{3,2,1,0:T(8,128)S(1)} %copy-done, s32[16,16,128]{2,1,0:T(8,128)S(1)} %copy-done.1), custom_call_target="tpu_custom_call" | custom-call | tf_op jit(solution)/shard_map/sweeps/pallas_call | solution.py:430
  30.3 0.7 %copy.4 = f32[16,16,128]{2,1,0:T(8,128)} copy(f32[16,16,128]{2,1,0:T(8,128)S(1)} %sweeps.1) | data formatting | bytes 262144
Async XLA Ops:
  0.0 1.0 %copy-start = (f32[3,16,16,128]{3,2,1,0:T(8,128)S(1)}, f32[3,16,16,128]{3,2,1,0:T(8,128)}, u32[]{:S(2)}) copy-start(f32[3,16,16,128]{3,2,1,0:T(8,128)} %src.1) | copy-start | bytes 1179652
  1.0 0.9 %copy-start.1 = (s32[16,16,128]{2,1,0:T(8,128)S(1)}, s32[16,16,128]{2,1,0:T(8,128)}, u32[]{:S(2)}) copy-start(s32[16,16,128]{2,1,0:T(8,128)} %lab.1) | copy-start | bytes 393220

commit v5 on v4

--- a/solution.py
+++ b/solution.py
@@ -230,6 +230,8 @@
         UP, DOWN, BOTH = (2, 4, 5), (3, 6, 7), (0, 1)
 
         def halo_start(k):
+            start_all([halo(k, s) for s in BOTH])
+
             @pl.when(has_up)
             def _():
                 start_all([halo(k, s) for s in UP])
@@ -237,8 +239,6 @@
             @pl.when(has_down)
             def _():
                 start_all([halo(k, s) for s in DOWN])
-
-            start_all([halo(k, s) for s in BOTH])
 
         def halo_arrive(k):
             for s in BOTH:
@@ -303,7 +303,7 @@
                 cz_low = z_down(cz)[:s_z]
                 cz = cz[:s_z]
                 cr = conduct(mi, r_up(mi, 1.0))
-                cr_low = conduct(mi, r_down(mi, 1.0))
+                cr_low = jnp.where(at_start[:s_z], 2.0 * mi / (mi + 1.0), pltpu.roll(cr, 1, 1))
                 fz = m * S[1, i]
                 fr = mi * S[2, i, :s_z]
                 flux = M[i + 1, :s_z] * S[0, i + 1, :s_z] - M[i - 1, :s_z] * S[0, i - 1, :s_z]

time: 31.1 us -> 31.1 us (level)
  no operation moved by 1% of the time
where the time goes in v5:
time: 31.1 us; the launch traced here: 31 us
  Pallas kernels  28.4 us (91%)
  local copies, waits for them, and re-layouts  2.56 us (8%)
    pallas_call x1, Pallas kernels, on_device(): make_kernel(sizes['phi'], sizes['row'], sizes['gz'], labels.shape)  28.4 us
    unnamed x5, local copies, waits for them, and re-layouts  2.56 us

profile of v5, /device:TPU:0, one launch (start us, length us, event | category | flops | bytes accessed | tf_op | source)
XLA Modules:
  0.0 31.0 jit_solution(6501386050836940002)
XLA Ops:
  0.0 0.0 copy-start
  0.0 1.0 %copy-done = f32[3,16,16,128]{3,2,1,0:T(8,128)S(1)} copy-done((f32[3,16,16,128]{3,2,1,0:T(8,128)S(1)}, f32[3,16,16,128]{3,2,1,0:T(8,128)}, u32[]{:S(2)}) %copy-start) | copy-done | bytes 393240
  1.0 0.0 copy-start.1
  1.0 0.9 %copy-done.1 = s32[16,16,128]{2,1,0:T(8,128)S(1)} copy-done((s32[16,16,128]{2,1,0:T(8,128)S(1)}, s32[16,16,128]{2,1,0:T(8,128)}, u32[]{:S(2)}) %copy-start.1) | copy-done | bytes 131096
  1.9 28.4 %sweeps.1 = f32[16,16,128]{2,1,0:T(8,128)S(1)} custom-call(f32[3,16,16,128]{3,2,1,0:T(8,128)S(1)} %copy-done, s32[16,16,128]{2,1,0:T(8,128)S(1)} %copy-done.1), custom_call_target="tpu_custom_call" | custom-call | tf_op jit(solution)/shard_map/sweeps/pallas_call | solution.py:430
  30.3 0.7 %copy.4 = f32[16,16,128]{2,1,0:T(8,128)} copy(f32[16,16,128]{2,1,0:T(8,128)S(1)} %sweeps.1) | data formatting | bytes 262144
Async XLA Ops:
  0.0 1.0 %copy-start = (f32[3,16,16,128]{3,2,1,0:T(8,128)S(1)}, f32[3,16,16,128]{3,2,1,0:T(8,128)}, u32[]{:S(2)}) copy-start(f32[3,16,16,128]{3,2,1,0:T(8,128)} %src.1) | copy-start | bytes 1179652
  1.0 0.9 %copy-start.1 = (s32[16,16,128]{2,1,0:T(8,128)S(1)}, s32[16,16,128]{2,1,0:T(8,128)}, u32[]{:S(2)}) copy-start(s32[16,16,128]{2,1,0:T(8,128)} %lab.1) | copy-start | bytes 393220

commit v6 on v5

--- a/solution.py
+++ b/solution.py
@@ -281,18 +281,28 @@
         for k in range(ITERS):
             cur = k % 2
 
+            def fresh(i, k=k, cur=cur):
+                new = wide_factor * U[k - 1, i]
+                if k > 1:
+                    new = new + Pot[1 - cur, i]
+                Pot[cur, i] = new
+                return new
+
             def perm_row(i, carry, k=k, cur=cur):
-                a, b = A[i], B[i]
-                here = Pot[cur, i]
-                s0 = S[0, i] - 0.5 * (Pot[cur, i + 1] - Pot[cur, i - 1])
+                before, here = carry
+                after = fresh(i + 1)
+                s0 = S[0, i] - 0.5 * (after - before)
                 s1 = S[1, i] - 0.5 * (z_up(here) - z_down(here))
                 s2 = S[2, i] - 0.5 * (r_up(here, 0.0) - r_down(here, 0.0))
                 field_sq = s0 * s0 + s1 * s1 + s2 * s2
-                M[i] = 1.0 + a / (1.0 + field_sq * b)
-                return carry
+                M[i] = 1.0 + A[i] / (1.0 + field_sq * B[i])
+                return here, after
 
             if k > 0:
-                lax.fori_loop(1, half + 3, perm_row, 0, unroll=True)
+                lax.fori_loop(1, half + 3, perm_row, (fresh(0), fresh(1)), unroll=True)
+                if k == ITERS - 1:
+                    give_potential = swap(Pot.at[cur, own_rows, whole_z, other_lanes], FP, 0)
+                    give_potential.start()
 
             def relax_row(i, carry, k=k, cur=cur):
                 below, acc = carry
@@ -354,17 +364,6 @@
                 halo_arrive(k)
                 wide_factor = jnp.broadcast_to(factor, (tall, wide))
 
-                def step(i, carry, k=k, cur=cur):
-                    new = wide_factor * U[k, i]
-                    if k > 0:
-                        new = new + Pot[cur, i]
-                    Pot[1 - cur, i] = new
-                    return carry
-
-                lax.fori_loop(0, half + 4, step, 0, unroll=True)
-                if k == ITERS - 2:
-                    give_potential = swap(Pot.at[1 - cur, own_rows, whole_z, other_lanes], FP, 0)
-                    give_potential.start()
             else:
                 wide_factor = jnp.broadcast_to(factor, (half, s_z, s_r))
                 out[pl.ds(half * c, half)] = (

time: 31.1 us -> 31.2 us (level)
  no operation moved by 1% of the time
where the time goes in v6:
time: 31.2 us; the launch traced here: 31 us
  Pallas kernels  28.4 us (91%)
  local copies, waits for them, and re-layouts  2.56 us (8%)
    pallas_call x1, Pallas kernels, on_device(): make_kernel(sizes['phi'], sizes['row'], sizes['gz'], labels.shape)  28.4 us
    unnamed x5, local copies, waits for them, and re-layouts  2.56 us

profile of v6, /device:TPU:0, one launch (start us, length us, event | category | flops | bytes accessed | tf_op | source)
XLA Modules:
  0.0 31.0 jit_solution(15657089842159679712)
XLA Ops:
  0.0 0.0 copy-start
  0.0 1.0 %copy-done = f32[3,16,16,128]{3,2,1,0:T(8,128)S(1)} copy-done((f32[3,16,16,128]{3,2,1,0:T(8,128)S(1)}, f32[3,16,16,128]{3,2,1,0:T(8,128)}, u32[]{:S(2)}) %copy-start) | copy-done | bytes 393240
  1.0 0.0 copy-start.1
  1.0 0.9 %copy-done.1 = s32[16,16,128]{2,1,0:T(8,128)S(1)} copy-done((s32[16,16,128]{2,1,0:T(8,128)S(1)}, s32[16,16,128]{2,1,0:T(8,128)}, u32[]{:S(2)}) %copy-start.1) | copy-done | bytes 131096
  1.9 28.4 %sweeps.1 = f32[16,16,128]{2,1,0:T(8,128)S(1)} custom-call(f32[3,16,16,128]{3,2,1,0:T(8,128)S(1)} %copy-done, s32[16,16,128]{2,1,0:T(8,128)S(1)} %copy-done.1), custom_call_target="tpu_custom_call" | custom-call | tf_op jit(solution)/shard_map/sweeps/pallas_call | solution.py:429
  30.3 0.7 %copy.4 = f32[16,16,128]{2,1,0:T(8,128)} copy(f32[16,16,128]{2,1,0:T(8,128)S(1)} %sweeps.1) | data formatting | bytes 262144
Async XLA Ops:
  0.0 1.0 %copy-start = (f32[3,16,16,128]{3,2,1,0:T(8,128)S(1)}, f32[3,16,16,128]{3,2,1,0:T(8,128)}, u32[]{:S(2)}) copy-start(f32[3,16,16,128]{3,2,1,0:T(8,128)} %src.1) | copy-start | bytes 1179652
  1.0 0.9 %copy-start.1 = (s32[16,16,128]{2,1,0:T(8,128)S(1)}, s32[16,16,128]{2,1,0:T(8,128)}, u32[]{:S(2)}) copy-start(s32[16,16,128]{2,1,0:T(8,128)} %lab.1) | copy-start | bytes 393220
